TPU v7x, 512 devices: a whole 4x8x8 slice. The times are simulated.
512 devices in a mesh: dp: 16 (over x, z_hi, core), seq: 32 (over y, z_lo).
Axes of the slice: x: 4, y: 8, z: 8 (z_hi: 2, z_lo: 4; z = z_hi * 4 + z_lo), core: 2. Of those that a mesh axis runs over, the one named last changes fastest.
Arguments:
- queries: bfloat16 [4096, 32, 128], P('seq', 'dp'), may hold values from -14 to 14
- keys: bfloat16 [4096, 32, 128], P('seq', 'dp'), may hold values from -14 to 14
- values: bfloat16 [4096, 32, 128], P('seq', 'dp'), may hold values from -6 to 6
- tan_queries: bfloat16 [4096, 32, 128], P('seq', 'dp'), may hold values from -6 to 6
- tan_keys: bfloat16 [4096, 32, 128], P('seq', 'dp'), may hold values from -6 to 6
- tan_values: bfloat16 [4096, 32, 128], P('seq', 'dp'), may hold values from -6 to 6
- gain_q: float32 [4096], P('dp'), may hold values from 0.7 to 2.5
- gain_k: float32 [4096], P('dp'), may hold values from 0.7 to 2.5
Outputs:
- primal_out: bfloat16 [4096, 32, 128], P('seq', 'dp')
- tangent_out: bfloat16 [4096, 32, 128], P('seq', 'dp')
All inputs are finite; a program needn't handle non-finite values.
Results may differ from a plain program's by a relative error of at most 0.012.
Values may be sent and summed in bfloat16 or wider, within the bound.
No kernel may reach another device: no remote copies, remote signals or barrier semaphores. Data moves between devices by JAX's collectives and lax.ppermute only.
A program may use at most 64 MiB of HBM per device.

v0:
```python
import math

import jax
import jax.numpy as jnp
from jax import lax
from jax.sharding import PartitionSpec as P

HS = 128
HEADS = 32


EPSILON = 1e-06


def norm_apply(primal, tangent, mean_square, cross_mean, gain):
    inverse = lax.rsqrt(mean_square + EPSILON)
    normed = gain * (primal * inverse)
    tan_normed = gain * (tangent * inverse - primal * (inverse * inverse * inverse) * cross_mean)
    return (normed.astype(jnp.bfloat16), tan_normed.astype(jnp.bfloat16))


def key_blocks(array):
    count = array.shape[0]
    block_rows = math.gcd(count, 512)
    return array.reshape(count // block_rows, block_rows, array.shape[1], array.shape[2])


def score_pair(query_heads, tan_query_heads, key_block, tan_key_block):
    factor = query_heads.shape[-1] ** (-0.5)
    scores = (
        jnp.einsum("hrd,phd->hrp", query_heads, key_block, preferred_element_type=jnp.float32)
        * factor
    )
    tan_scores = (
        jnp.einsum("hrd,phd->hrp", tan_query_heads, key_block, preferred_element_type=jnp.float32)
        + jnp.einsum("hrd,phd->hrp", query_heads, tan_key_block, preferred_element_type=jnp.float32)
    ) * factor
    return (scores, tan_scores)


def shards(queries, keys, values, tan_queries, tan_keys, tan_values, gain_q, gain_k):
    local_rows, local_heads, head_size = queries.shape
    feature_total = HEADS * HS

    def flat_float(array):
        return array.reshape(local_rows, local_heads * head_size).astype(jnp.float32)

    q_float, tq_float = (flat_float(queries), flat_float(tan_queries))
    k_float, tk_float = (flat_float(keys), flat_float(tan_keys))
    sums = lax.psum(
        (
            jnp.sum(q_float * q_float, axis=-1, keepdims=True),
            jnp.sum(q_float * tq_float, axis=-1, keepdims=True),
            jnp.sum(k_float * k_float, axis=-1, keepdims=True),
            jnp.sum(k_float * tk_float, axis=-1, keepdims=True),
        ),
        "dp",
    )
    normed_q, normed_tq = norm_apply(
        q_float, tq_float, sums[0] / feature_total, sums[1] / feature_total, gain_q
    )
    normed_k, normed_tk = norm_apply(
        k_float, tk_float, sums[2] / feature_total, sums[3] / feature_total, gain_k
    )
    shard_shape = queries.shape
    normed_q = normed_q.reshape(shard_shape)
    normed_tq = normed_tq.reshape(shard_shape)
    normed_k = normed_k.reshape(shard_shape)
    normed_tk = normed_tk.reshape(shard_shape)
    query_heads = normed_q.transpose(1, 0, 2)
    tan_query_heads = normed_tq.transpose(1, 0, 2)
    stat_shape = (local_heads, local_rows, 1)
    start_state = (
        jnp.full(stat_shape, -jnp.inf, jnp.float32),
        jnp.zeros(stat_shape, jnp.float32),
        jnp.zeros(stat_shape, jnp.float32),
    )
    pieces = (
        lax.all_gather(normed_k, "seq", axis=0, tiled=True),
        lax.all_gather(normed_tk, "seq", axis=0, tiled=True),
    )

    def step(state, blocks):
        high, total, cross = state
        scores, tan_scores = score_pair(query_heads, tan_query_heads, blocks[0], blocks[1])
        new_high = jnp.maximum(high, jnp.max(scores, axis=-1, keepdims=True))
        rescale = jnp.exp(high - new_high)
        shifted = jnp.exp(scores - new_high)
        return (
            (
                new_high,
                total * rescale + jnp.sum(shifted, axis=-1, keepdims=True),
                cross * rescale + jnp.sum(shifted * tan_scores, axis=-1, keepdims=True),
            ),
            None,
        )

    state, unused = lax.scan(step, start_state, (key_blocks(pieces[0]), key_blocks(pieces[1])))
    row_max, totals, cross = state
    mean_tangent = cross / totals
    empty = jnp.zeros((local_heads, local_rows, head_size), jnp.float32)
    pieces = (
        lax.all_gather(normed_k, "seq", axis=0, tiled=True),
        lax.all_gather(normed_tk, "seq", axis=0, tiled=True),
        lax.all_gather(values, "seq", axis=0, tiled=True),
        lax.all_gather(tan_values, "seq", axis=0, tiled=True),
    )

    def step(state, blocks):
        out_sum, tan_sum = state
        key_block, tan_key_block, value_block, tan_value_block = blocks
        scores, tan_scores = score_pair(query_heads, tan_query_heads, key_block, tan_key_block)
        weights = jnp.exp(scores - row_max) / totals
        weights_low = weights.astype(jnp.bfloat16)
        tan_low = (weights * (tan_scores - mean_tangent)).astype(jnp.bfloat16)
        out_sum = out_sum + jnp.einsum(
            "hrp,phd->hrd", weights_low, value_block, preferred_element_type=jnp.float32
        )
        tan_sum = tan_sum + jnp.einsum(
            "hrp,phd->hrd", tan_low, value_block, preferred_element_type=jnp.float32
        )
        tan_sum = tan_sum + jnp.einsum(
            "hrp,phd->hrd", weights_low, tan_value_block, preferred_element_type=jnp.float32
        )
        return ((out_sum, tan_sum), None)

    state, unused = lax.scan(
        step,
        (empty, empty),
        (
            key_blocks(pieces[0]),
            key_blocks(pieces[1]),
            key_blocks(pieces[2]),
            key_blocks(pieces[3]),
        ),
    )
    out_sum, tan_sum = state
    primal_out = out_sum.transpose(1, 0, 2).astype(jnp.bfloat16)
    tangent_out = tan_sum.transpose(1, 0, 2).astype(jnp.bfloat16)
    return (primal_out, tangent_out)


def solution(mesh):
    return jax.shard_map(
        shards,
        mesh=mesh,
        in_specs=(
            P("seq", "dp", None),
            P("seq", "dp", None),
            P("seq", "dp", None),
            P("seq", "dp", None),
            P("seq", "dp", None),
            P("seq", "dp", None),
            P("dp"),
            P("dp"),
        ),
        out_specs=(P("seq", "dp", None), P("seq", "dp", None)),
        check_vma=False,
    )
```

profile of v0, /device:TPU:2, one launch (start us, length us, event | category | flops | bytes accessed | tf_op | source)
XLA Modules:
  0.0 761.3 jit_solution(1219201520382262955)
XLA Ops:
  7.2 1.0 fusion.60
  8.2 1.0 fusion.65
  9.2 46.4 %all-reduce = (f32[128,1]{0,1:T(1,128)S(1)}, f32[128,1]{0,1:T(1,128)S(1)}, f32[128,1]{0,1:T(1,128)S(1)}, f32[128,1]{0,1:T(1,128)S(1)}) all-reduce(f32[128,1]{0,1:T(1,128)S(1)} %bitcast.145, f32[128,1]{0,1:T(1,128)S(1)} %bitcast.147, f32[128,1]{0,1:T(1,128)S(1)} %bitcast.146, ...), channel_id=1, replica_groups=mesh['dp'=16,'seq'=32] {'dp'}, use_global_device_ids=true, to_apply=%region_1.0 | all-reduce | flops 512 | bytes 4096 | tf_op jit(solution)/shard_map/psum | solution.py:50
  55.6 1.7 fusion.55
  57.3 0.7 all-gather.7.cloned.1.call-update
  58.1 1.5 copy.27
  59.6 1.5 copy.28
  61.2 1.0 fusion.67
  62.2 153.9 %all-gather.5.cloned.1.call-done = bf16[4096,2,128]{2,0,1:T(8,128)(2,1)} async-done(((bf16[128,2,128]{2,0,1:T(8,128)(2,1)}), bf16[4096,2,128]{2,0,1:T(8,128)(2,1)}) %all-gather.5.cloned.1.call-update) | async-done | bytes 2097168 | tf_op jit(solution)/shard_map/all_gather | solution.py:103
  216.1 1.7 copy.29
  217.8 156.6 %all-gather.7.cloned.1.call-done = bf16[4096,2,128]{2,0,1:T(8,128)(2,1)} async-done(((bf16[128,2,128]{2,0,1:T(8,128)(2,1)}), bf16[4096,2,128]{2,0,1:T(8,128)(2,1)}) %all-gather.7.cloned.1.call-update) | async-done | bytes 2097168 | tf_op jit(solution)/shard_map/all_gather | solution.py:104
  374.4 14.9 %while.28 = (s32[]{:T(128)}, f32[2,128,1]{1,0,2:T(2,128)S(1)}, f32[2,128,1]{1,0,2:T(2,128)S(1)}, f32[2,128,1]{1,0,2:T(2,128)S(1)}, bf16[8,512,2,128]{3,1,2,0:T(8...) while((s32[]{:T(128)}, f32[2,128,1]{1,0,2:T(2,128)S(1)}, ...), condition=%wide.region_12.13_spmd.clone, body=%wide.region_8.12_spmd.clone.sunk | while | flops 101844736 | bytes 3623544 | solution.py:98
  374.9 1.2 fusion.110
  376.8 1.2 fusion.110
  378.6 1.2 fusion.110
  380.5 1.2 fusion.110
  382.3 1.2 fusion.110
  384.2 1.2 fusion.110
  386.1 1.2 fusion.110
  387.9 1.2 fusion.110
  389.3 142.9 %all-gather.9.cloned.1.call-done = bf16[4096,2,128]{2,0,1:T(8,128)(2,1)} async-done(((bf16[128,2,128]{2,0,1:T(8,128)(2,1)}), bf16[4096,2,128]{2,0,1:T(8,128)(2,1)}) %all-gather.9.cloned.1.call-update) | async-done | bytes 2097168 | tf_op jit(solution)/shard_map/all_gather | solution.py:105
  532.2 157.6 %all-gather.11.cloned.1.call-done = bf16[4096,2,128]{2,0,1:T(8,128)(2,1)} async-done(((bf16[128,2,128]{2,0,1:T(8,128)(2,1)}), bf16[4096,2,128]{2,0,1:T(8,128)(2,1)}) %all-gather.11.cloned.1.call-update) | async-done | bytes 2097168 | tf_op jit(solution)/shard_map/all_gather | solution.py:106
  689.7 61.7 %while.29 = (s32[]{:T(128)}, f32[2,128,128]{2,1,0:T(8,128)}, f32[2,128,128]{2,1,0:T(8,128)}, bf16[8,512,2,128]{3,1,2,0:T(8,128)(2,1)S(1)}, bf16[2,128,128]{2,1,0...) while((s32[]{:T(128)}, f32[2,128,128]{2,1,0:T(8,128)}, ...), condition=%wide.region_14.15_spmd.clone, body=%wide.region_13.14_spmd.clone.sunk | while | flops 202801152 | bytes 6754972 | solution.py:127
  690.0 1.9 fusion.124
  692.1 1.0 constant_dynamic-slice_fusion.2
  693.1 0.3 copy.69
  693.4 2.1 fusion.126
  695.5 1.9 convolution_add_fusion.4
  697.6 1.9 fusion.124
  699.7 1.0 constant_dynamic-slice_fusion.2
  700.7 0.3 copy.69
  701.0 2.2 fusion.126
  703.2 1.9 convolution_add_fusion.4
  705.4 1.9 fusion.124
  707.5 1.0 constant_dynamic-slice_fusion.2
  708.5 0.3 copy.69
  708.7 2.2 fusion.126
  710.9 1.9 convolution_add_fusion.4
  713.1 1.9 fusion.124
  715.2 1.0 constant_dynamic-slice_fusion.2
  716.2 0.3 copy.69
  716.5 2.2 fusion.126
  718.7 1.9 convolution_add_fusion.4
  720.8 1.9 fusion.124
  722.9 1.0 constant_dynamic-slice_fusion.2
  723.9 0.3 copy.69
  724.2 2.2 fusion.126
  726.4 1.9 convolution_add_fusion.4
  728.6 1.9 fusion.124
  730.7 1.0 constant_dynamic-slice_fusion.2
  731.9 2.2 fusion.126
  734.1 1.9 convolution_add_fusion.4
  736.3 1.9 fusion.124
  738.4 1.0 constant_dynamic-slice_fusion.2
  739.7 2.2 fusion.126
  741.8 1.9 convolution_add_fusion.4
  744.0 1.9 fusion.124
  746.1 1.0 constant_dynamic-slice_fusion.2
  747.4 2.2 fusion.126
  749.6 1.9 convolution_add_fusion.4
  751.5 0.9 convert_element_type.75
  752.4 0.7 copy.64
  753.1 0.9 convert_element_type.74
  754.0 0.7 copy.65
  (82 shorter events, 9.5 us)
Async XLA Ops:
  7.2 208.9 %all-gather.5.cloned.1.call-start = ((), (), s32[]{:S(2)}) async-start(), calls=%async_computation | async-start | bytes 2162688 | tf_op jit(solution)/shard_map/all_gather | solution.py:103
  57.3 317.1 %all-gather.7.cloned.1.call-start = ((), (), s32[]{:S(2)}) async-start(), calls=%async_computation.1 | async-start | bytes 2162688 | tf_op jit(solution)/shard_map/all_gather | solution.py:104
  58.1 474.1 %all-gather.9.cloned.1.call-start = ((), (), s32[]{:S(2)}) async-start(), calls=%async_computation.2 | async-start | bytes 2162688 | tf_op jit(solution)/shard_map/all_gather | solution.py:105
  59.6 630.2 %all-gather.11.cloned.1.call-start = ((), (), s32[]{:S(2)}) async-start(), calls=%async_computation.3 | async-start | bytes 2162688 | tf_op jit(solution)/shard_map/all_gather | solution.py:106
Sparse Core Ops, SparseCore 0:
  57.4 158.6 all-gather.4
  218.8 155.6 all-gather.6
  376.5 155.6 all-gather.8
  534.1 155.6 all-gather.10
where the time goes:
time: 763 us; the launch traced here: 761 us
  waiting for transfers between devices  612 us (80%)
  matrix products  65 us (9%)
  blocking collectives  46.4 us (6%)
  local copies, waits for them, and re-layouts  16.1 us (2%)
  between operations  13.9 us (2%)
    all_gather x1, waiting for transfers between devices, shards(): lax.all_gather(tan_values, 'seq', axis=0, tiled=True)  158 us
    all_gather x1, waiting for transfers between devices, shards(): lax.all_gather(normed_tk, 'seq', axis=0, tiled=True)  157 us
    all_gather x1, waiting for transfers between devices, shards(): lax.all_gather(normed_k, 'seq', axis=0, tiled=True)  154 us
    all_gather x1, waiting for transfers between devices, shards(): lax.all_gather(values, 'seq', axis=0, tiled=True)  143 us
    psum x1, blocking collectives, shards(): lax.psum((jnp.sum(q_float * q_float, axis=-1, keepdims=True), jnp.sum(q_f...  46.4 us
    dot_general x8, matrix products, step(): jnp.einsum('hrp,phd->hrd', tan_low, value_block, preferred_element_type=j...  17.3 us
    dot_general x8, matrix products, step(): jnp.einsum('hrp,phd->hrd', weights_low, value_block, preferred_element_ty...  15.3 us
  transfers between devices with their start and end apart: 4, of which 4 were waited for; matrix products, arithmetic and copies ran while one was open for 3% of the time, Pallas kernels for 0%

commit v1 on v0

v1 whole, which is shorter than its diff:
```python
import functools
import math

import jax
import jax.numpy as jnp
from jax import lax
from jax.experimental import pallas as pl
from jax.experimental.pallas import tpu as pltpu
from jax.sharding import PartitionSpec as P

HS = 128
HEADS = 32
FEATURES = HEADS * HS
EPSILON = 1e-06
FACTOR = HS**-0.5
LOG2E = math.log2(math.e)

Y, Z, DP = 8, 4, 16
ROWS = 128
LOCAL = 2
PART = 528

Z_GROUPS = [[y * Z + z for z in range(Z)] for y in range(Y)]
Y_GROUPS = [[y * Z + z for y in range(Y)] for z in range(Z)]

VMEM_LIMIT = 40 * 1024 * 1024
VMEM_WHOLE = 60 * 1024 * 1024
SMALL = pl.CostEstimate(flops=1, bytes_accessed=1, transcendentals=0)


def params(limit=VMEM_LIMIT):
    return pltpu.CompilerParams(vmem_limit_bytes=limit)


def swaps(size, bits):
    return [(i, i ^ bits) for i in range(size)]


def loader(refs, raw, wide, sems):
    loads = [pltpu.make_async_copy(ref, raw.at[i], sems.at[i]) for i, ref in enumerate(refs)]
    for load in loads:
        load.start()

    def heads(i):
        loads[i].wait()
        wide[i] = raw[i].astype(jnp.float32)
        return [wide[i, pl.ds(h, ROWS, stride=LOCAL), :] for h in range(LOCAL)]

    return heads


def stats_kernel(q, k, tq, tk, gain_q, gain_k, stat_out, scaled_out, raw, wide, gains, sems):
    gain_loads = [
        pltpu.make_async_copy(ref, gains.at[i], sems.at[4 + i])
        for i, ref in enumerate((gain_q, gain_k))
    ]
    for load in gain_loads:
        load.start()
    heads = loader((q, tq, k, tk), raw, wide, sems)
    pairs = [heads(i) for i in range(4)]
    for load in gain_loads:
        load.wait()
    rows = []
    for i in (0, 1):
        primal, tangent = pairs[2 * i], pairs[2 * i + 1]
        for other in (primal, tangent):
            product = primal[0] * other[0] + primal[1] * other[1]
            rows.append(jnp.sum(product.T, axis=0, keepdims=True))
        if i == 0:
            for h in range(LOCAL):
                scaled_out[0, h, 0:ROWS] = gains[0, h : h + 1] * primal[h]
                scaled_out[1, h, 0:ROWS] = gains[0, h : h + 1] * tangent[h]
                tail = jnp.broadcast_to(gains[1, h : h + 1], (8, HS))
                scaled_out[0, h, ROWS:] = tail
                scaled_out[1, h, ROWS:] = tail
    stat_out[...] = jnp.broadcast_to(jnp.concatenate(rows, axis=0)[None], stat_out.shape)


def split_three(x):
    high = x.astype(jnp.bfloat16).astype(jnp.float32)
    rest = x - high
    middle = rest.astype(jnp.bfloat16).astype(jnp.float32)
    return [high, middle, rest - middle]


def bulk_kernel(k, tk, v, tv, out, raw, wide, packed, sems):
    heads = loader((k, tk, v, tv), raw, wide, sems)
    for i in range(4):
        for h, block in enumerate(heads(i)):
            block = block if i < 2 else block.T
            packed[h, i * 128 : (i + 1) * 128] = block.astype(jnp.bfloat16)
    send = pltpu.make_async_copy(packed, out, sems.at[4])
    send.start()
    send.wait()


def inverse_and_cross(squares, crosses):
    inverse = lax.rsqrt(squares * (1.0 / FEATURES) + EPSILON)
    cross = inverse * inverse * inverse * (crosses * (1.0 / FEATURES))
    return [jnp.broadcast_to(row, (ROWS, ROWS)).T for row in (inverse, cross)]


def norm_kernel(parts, scaled, q_out, key_out, gain_out):
    bf16 = jnp.bfloat16
    stats = jnp.sum(parts[...], axis=0)
    inverse, cross = inverse_and_cross(stats[0:1], stats[1:2])
    for h in range(LOCAL):
        primal, tangent = scaled[0, h, 0:ROWS], scaled[1, h, 0:ROWS]
        gain_out[h] = scaled[0, h, ROWS:]
        q_out[h, 0:128] = (primal * inverse).astype(bf16)
        q_out[h, 128:256] = (tangent * inverse - primal * cross).astype(bf16)
    key_out[...] = jnp.broadcast_to(stats[2:4][None], key_out.shape)


def stack_rows(rows, cols):
    index = lax.broadcasted_iota(jnp.int32, (16, cols), 0)
    tile = jnp.zeros((16, cols), jnp.float32)
    for i, row in enumerate(rows):
        tile = jnp.where(index == i, row, tile)
    return tile.astype(jnp.bfloat16)


def coef_kernel(sums, gains, coef):
    for y in range(Y):
        inverse, cross = inverse_and_cross(sums[y, 0:1], sums[y, 1:2])
        for h in range(LOCAL):
            coef[0, y, h] = inverse * gains[h, 0:1]
            coef[1, y, h] = cross * gains[h, 0:1]


def attend_kernel(count, bulk, normed, *refs):
    f32, bf16 = jnp.float32, jnp.bfloat16
    queries, outs, (s_ref, t_ref) = refs[:count], refs[count : 2 * count], refs[-2:]
    if count > 1:
        coef, normed = normed, refs[2 * count]
        for h in range(LOCAL):
            for y in range(Y):
                key = bulk[y, h, 0:128].astype(f32)
                tan_key = bulk[y, h, 128:256].astype(f32)
                normed[y, h, 0:128] = (key * coef[0, y, h]).astype(bf16)
                normed[y, h, 128:256] = (tan_key * coef[0, y, h] - key * coef[1, y, h]).astype(bf16)
    nt = (((1,), (1,)), ((), ()))
    cols = count * ROWS

    rows = []
    for h in range(LOCAL):
        query = jnp.concatenate([q[h, 0:128] for q in queries], axis=0)
        tan_query = jnp.concatenate([q[h, 128:256] for q in queries], axis=0)
        both = jnp.concatenate([tan_query, query], axis=1)
        high = None
        for start in range(0, Y, 4):
            key = jnp.concatenate([normed[y, h, 0:128] for y in range(start, start + 4)], axis=0)
            score = lax.dot_general(key, query, nt, preferred_element_type=f32)
            for i, y in enumerate(range(start, start + 4)):
                scaled = score[i * 128 : (i + 1) * 128] * (FACTOR * LOG2E)
                s_ref[y] = scaled
                block_high = jnp.max(scaled.reshape(16, 8, cols), axis=0)
                high = block_high if high is None else jnp.maximum(high, block_high)
        high = jnp.max(high, axis=0, keepdims=True)
        total = jnp.zeros((8, cols), f32)
        cross = jnp.zeros((8, cols), f32)
        out = jnp.zeros((HS, cols), f32)
        tangent = jnp.zeros((HS, cols), f32)
        for start in range(0, Y, 2):
            pair = range(start, start + 2)
            keys = jnp.concatenate(
                [
                    jnp.concatenate([normed[y, h, first : first + 128] for y in pair], axis=0)
                    for first in (0, 128)
                ],
                axis=1,
            )
            tan = lax.dot_general(keys, both, nt, preferred_element_type=f32)
            lows = []
            for i, y in enumerate(pair):
                scaled = s_ref[y]
                weight = jnp.exp2(scaled - high)
                tan_score = tan[i * 128 : (i + 1) * 128] * FACTOR
                s_ref[y] = weight
                t_ref[y] = tan_score
                total = total + jnp.sum(weight.reshape(16, 8, cols), axis=0)
                cross = cross + jnp.sum((weight * tan_score).reshape(16, 8, cols), axis=0)
                lows.append(weight.astype(bf16))
            values = jnp.concatenate(
                [
                    jnp.concatenate([bulk[y, h, first : first + 128] for y in pair], axis=1)
                    for first in (256, 384)
                ],
                axis=0,
            )
            sums = jnp.dot(values, jnp.concatenate(lows, axis=0), preferred_element_type=f32)
            out = out + sums[0:128]
            tangent = tangent + sums[128:256]
        total = jnp.sum(total, axis=0, keepdims=True)
        inverse = 1.0 / total
        mean = jnp.sum(cross, axis=0, keepdims=True) * inverse
        for start in range(0, Y, 2):
            pair = range(start, start + 2)
            tan_lows = [(s_ref[y] * (t_ref[y] - mean)).astype(bf16) for y in pair]
            tangent = tangent + jnp.dot(
                jnp.concatenate([bulk[y, h, 256:384] for y in pair], axis=1),
                jnp.concatenate(tan_lows, axis=0),
                preferred_element_type=f32,
            )
        out = (out * inverse).astype(bf16)
        tangent = (tangent * inverse).astype(bf16)
        rows += split_three(high + jnp.log2(total)) + split_three(mean)
        for i, ref in enumerate(outs):
            lanes = slice(i * ROWS, (i + 1) * ROWS)
            ref[h * 256 : h * 256 + 128] = out[:, lanes]
            ref[h * 256 + 128 : h * 256 + 256] = tangent[:, lanes]
    stats = stack_rows(rows, cols)
    for i, ref in enumerate(outs):
        ref[512:PART] = stats[:, i * ROWS : (i + 1) * ROWS]
        if ref.shape[0] > PART:
            ref[PART:] = jnp.zeros((ref.shape[0] - PART, HS), bf16)


def merge_kernel(p0, p1, p2, p3, out_ref, tan_ref, wide):
    f32, bf16 = jnp.float32, jnp.bfloat16
    for h in range(LOCAL):
        parts = (p0, p1, p2, p3)
        logs, means = [], []
        for z in range(Z):
            stats = parts[z][512:528].astype(f32)[6 * h : 6 * h + 6]
            logs.append(stats[0:1] + stats[1:2] + stats[2:3])
            means.append(stats[3:4] + stats[4:5] + stats[5:6])
        top = jnp.maximum(jnp.maximum(logs[0], logs[1]), jnp.maximum(logs[2], logs[3]))
        weights = [jnp.exp2(x - top) for x in logs]
        inverse = 1.0 / (weights[0] + weights[1] + weights[2] + weights[3])
        weights = [w * inverse for w in weights]
        mean = sum(w * m for w, m in zip(weights, means))
        out = jnp.zeros((HS, ROWS), f32)
        tangent = jnp.zeros((HS, ROWS), f32)
        for z in range(Z):
            piece = parts[z][h * 256 : h * 256 + 128].astype(f32)
            out = out + weights[z] * piece
            tangent = tangent + weights[z] * parts[z][h * 256 + 128 : h * 256 + 256].astype(f32)
            tangent = tangent + (weights[z] * (means[z] - mean)) * piece
        wide[0, pl.ds(h, ROWS, stride=LOCAL), :] = out.T
        wide[1, pl.ds(h, ROWS, stride=LOCAL), :] = tangent.T
    out_ref[...] = wide[0].astype(bf16)
    tan_ref[...] = wide[1].astype(bf16)


def shards(queries, keys, values, tan_queries, tan_keys, tan_values, gain_q, gain_k):
    f32, bf16 = jnp.float32, jnp.bfloat16
    flat = lambda x: x.reshape(ROWS * LOCAL, HS)
    q, k, v = flat(queries), flat(keys), flat(values)
    tq, tk, tv = flat(tan_queries), flat(tan_keys), flat(tan_values)
    raw = lambda n: pltpu.VMEM((n, ROWS * LOCAL, HS), bf16)
    wide = lambda n: pltpu.VMEM((n, ROWS * LOCAL, HS), f32)
    hbm = pl.BlockSpec(memory_space=pltpu.HBM)
    vmem = pl.BlockSpec(memory_space=pltpu.VMEM)
    struct = jax.ShapeDtypeStruct
    block = (Y, LOCAL, 256, HS)

    stats, scaled = pl.pallas_call(
        stats_kernel,
        out_shape=(struct((DP, 4, ROWS), f32), struct((2, LOCAL, ROWS + 8, HS), f32)),
        in_specs=[hbm] * 6,
        out_specs=(vmem, vmem),
        scratch_shapes=[
            raw(4),
            wide(4),
            pltpu.VMEM((2, LOCAL, HS), f32),
            pltpu.SemaphoreType.DMA((6,)),
        ],
        compiler_params=params(VMEM_WHOLE),
        cost_estimate=SMALL,
        name="stats",
    )(q, k, tq, tk, gain_q.reshape(LOCAL, HS), gain_k.reshape(LOCAL, HS))
    bulk = pl.pallas_call(
        bulk_kernel,
        out_shape=struct((LOCAL, 512, HS), bf16),
        in_specs=[hbm] * 4,
        out_specs=hbm,
        scratch_shapes=[
            raw(4),
            wide(4),
            pltpu.VMEM((LOCAL, 512, HS), bf16),
            pltpu.SemaphoreType.DMA((5,)),
        ],
        compiler_params=params(VMEM_WHOLE),
        cost_estimate=SMALL,
        name="bulk",
    )(k, tk, v, tv)
    bulk = lax.all_gather(bulk, "seq", axis_index_groups=Y_GROUPS)
    stats = lax.all_to_all(stats, "dp", 0, 0)
    q_mine, sums, gains = pl.pallas_call(
        norm_kernel,
        out_shape=(
            struct((LOCAL, 256, HS), bf16),
            struct((Y, 2, ROWS), f32),
            struct((LOCAL, 8, HS), f32),
        ),
        compiler_params=params(),
        cost_estimate=SMALL,
        name="norm",
    )(stats, scaled)
    sums = lax.all_to_all(sums, "seq", 0, 0, axis_index_groups=Y_GROUPS)
    trade = lambda x, i: lax.ppermute(x, "seq", swaps(Y * Z, i))
    queries_of = [q_mine] + [trade(q_mine, i) for i in (1, 2, 3)]
    coef = pl.pallas_call(
        coef_kernel,
        out_shape=struct((2, Y, LOCAL, ROWS, HS), f32),
        compiler_params=params(),
        cost_estimate=pl.CostEstimate(flops=1_000_000_000, bytes_accessed=1, transcendentals=0),
        name="coef",
    )(sums, gains)

    def attend(bulk, scales, *blocks):
        count = len(blocks)
        spare = 16 if count > 1 else 0
        return pl.pallas_call(
            functools.partial(attend_kernel, count),
            out_shape=(struct((PART + spare, HS), bf16),) * count
            + (struct((Y, LOCAL, 256, HS), bf16),) * (count > 1),
            scratch_shapes=[pltpu.VMEM((Y, ROWS, count * ROWS), f32)] * 2,
            compiler_params=params(),
            cost_estimate=pl.CostEstimate(
                flops=402_653_184 * count, bytes_accessed=4_000_000, transcendentals=262_144 * count
            ),
            name="attend" + "".join(map(str, blocks)),
        )(bulk, scales, *[queries_of[i] for i in blocks])

    part2, part3, normed = attend(bulk, coef, 2, 3)
    bulk, part2, part3 = lax.optimization_barrier((bulk, part2, part3))
    (part1,) = attend(bulk, normed, 1)
    bulk, part1 = lax.optimization_barrier((bulk, part1))
    (part0,) = attend(bulk, normed, 0)
    parts = [part0, trade(part1, 1), trade(part2, 2), trade(part3, 3)]
    out, tangent = pl.pallas_call(
        merge_kernel,
        out_shape=(struct((ROWS * LOCAL, HS), bf16),) * 2,
        scratch_shapes=[wide(2)],
        compiler_params=params(),
        cost_estimate=SMALL,
        name="merge",
    )(*parts)
    shape = queries.shape
    return (out.reshape(shape), tangent.reshape(shape))


def solution(mesh):
    token = P("seq", "dp", None)
    return jax.shard_map(
        shards,
        mesh=mesh,
        in_specs=(token,) * 6 + (P("dp"), P("dp")),
        out_specs=(token, token),
        check_vma=False,
    )
```

time: 763 us -> 86.3 us (0.11)
  waiting for transfers between devices: 612 us -> 9.92 us
  matrix products: 65 us -> 0 us
  starting transfers between devices: 0.16 us -> 26.8 us
  blocking collectives: 46.4 us -> 21.9 us
  local copies, waits for them, and re-layouts: 16.1 us -> 2.55 us
  Pallas kernels: 0 us -> 10.3 us
    all_gather x4 -> x1, waiting for transfers between devices: 611 us -> 0.92 us  [shards(): bulk = lax.all_gather(bulk, 'seq', axis_index_groups=Y_GROUPS)]
    dot_general x64 -> x0, matrix products: 65 us -> none  [the longest x8 17.3 us: step(): jnp.einsum('hrp,phd->hrd', tan_low, value_block, preferred_element_type=j...]
    psum x1 -> x0, blocking collectives: 46.4 us -> none  [shards(): lax.psum((jnp.sum(q_float * q_float, axis=-1, keepdims=True), jnp.sum(q_f...]
    all_to_all x0 -> x1, blocking collectives: none -> 21.9 us  [shards(): stats = lax.all_to_all(stats, 'dp', 0, 0)]
    ppermute x0 -> x6, starting transfers between devices: none -> 19.7 us  [shards(): trade = lambda x, i: lax.ppermute(x, 'seq', swaps(Y * Z, i))]
    pallas_call x0 -> x8, Pallas kernels: none -> 10.3 us  [the longest x3 4.73 us: attend(): pl.pallas_call(functools.partial(attend_kernel, count), out_shape=(struct...]
    dynamic_slice x16 -> x0, local copies, waits for them, and re-layouts: 10 us -> none  [shards(): lax.scan(step, start_state, (key_blocks(pieces[0]), key_blocks(pieces[1])))]
  transfers between devices with their start and end apart: 4 -> 8, of which waited for: 4 -> 3; matrix products, arithmetic and copies ran while one was open for 3% -> 0% of each run, Pallas kernels for 0% -> 9%
where the time goes in v1:
time: 86.3 us; the launch traced here: 85.7 us
  starting transfers between devices  26.8 us (31%)
  blocking collectives  21.9 us (25%)
  between operations  14.1 us (16%)
  Pallas kernels  10.3 us (12%)
  waiting for transfers between devices  9.92 us (11%)
  local copies, waits for them, and re-layouts  2.55 us (3%)
    all_to_all x1, blocking collectives, shards(): stats = lax.all_to_all(stats, 'dp', 0, 0)  21.9 us
    ppermute x6, starting transfers between devices, shards(): trade = lambda x, i: lax.ppermute(x, 'seq', swaps(Y * Z, i))  19.7 us
    all_to_all x1, starting transfers between devices, shards(): sums = lax.all_to_all(sums, 'seq', 0, 0, axis_index_groups=Y_GROUPS)  7.12 us
    all_to_all x1, waiting for transfers between devices, shards(): sums = lax.all_to_all(sums, 'seq', 0, 0, axis_index_groups=Y_GROUPS)  5.88 us
    pallas_call x3, Pallas kernels, attend(): pl.pallas_call(functools.partial(attend_kernel, count), out_shape=(struct...  4.73 us
    ppermute x6, waiting for transfers between devices, shards(): trade = lambda x, i: lax.ppermute(x, 'seq', swaps(Y * Z, i))  3.1 us
    unnamed x6, local copies, waits for them, and re-layouts  2.55 us
    pallas_call x1, Pallas kernels, shards(): pl.pallas_call(bulk_kernel, out_shape=struct((LOCAL, 512, HS), bf16), in_...  1.88 us
  transfers between devices with their start and end apart: 8, of which 3 were waited for; matrix products, arithmetic and copies ran while one was open for 0% of the time, Pallas kernels for 9%

profile of v1, /device:TPU:2, one launch (start us, length us, event | category | flops | bytes accessed | tf_op | source)
XLA Modules:
  0.0 85.7 jit_solution(10712249373029663663)
XLA Ops:
  7.2 0.0 all-gather.3.cloned.1.call-start
  7.2 1.9 %bulk.1 = bf16[2,512,128]{2,1,0:T(8,128)(2,1)} custom-call(bf16[256,128]{1,0:T(8,128)(2,1)} %bitcast.14, bf16[256,128]{1,0:T(8,128)(2,1)} %bitcast.16, bf16[256,128]{1,0:T(8,128)(2,1)} %bitcast.20, bf16[256,128]{1,0:T(8,128)(2,1)} %bitcast.21), custom_call_target="tpu_custom_call" | custom-call | flops 1 | bytes 1 | tf_op jit(solution)/shard_map/bulk/pallas_call | solution.py:273
  9.1 0.0 all-gather.3.cloned.1.call-update
  9.1 1.8 %stats.1 = (f32[16,4,128]{2,1,0:T(4,128)}, f32[2,2,136,128]{3,2,1,0:T(8,128)}) custom-call(bf16[256,128]{1,0:T(8,128)(2,1)} %bitcast.18, bf16[256,128]{1,0:T(8,128)(2,1)} %bitcast.15, bf16[256,128]{1,0:T(8,128)(2,1)} %bitcast.19, bf16[256,128]{1,0:T(8,128)(2,1)} %bitcast.17, f32[2,128]{1,0:T(2,128)} %bitcast.22, f32[2,128]{1,0:T(2,128)} %bitcast.23), custom_call_target="tpu_custom_call" | custom-call | flops 1 | bytes 1 | tf_op jit(solution)/shard_map/stats/pallas_call | solution.py:258
  11.0 21.9 %all_to_all.10.parts = f32[16,4,128]{2,1,0:T(4,128)S(1)} all-to-all(f32[16,4,128]{2,1,0:T(4,128)} %get-tuple-element.17), channel_id=1, replica_groups=mesh['dp'=16,'seq'=32] {'dp'}, dimensions={0} | all-to-all | bytes 65536 | tf_op jit(solution)/shard_map/all_to_all | solution.py:289
  32.9 0.0 copy-start.2
  32.9 1.0 %copy-done.2 = f32[2,2,136,128]{3,2,1,0:T(8,128)S(1)} copy-done((f32[2,2,136,128]{3,2,1,0:T(8,128)S(1)}, f32[2,2,136,128]{3,2,1,0:T(8,128)}, u32[]{:S(2)}) %copy-start.2) | copy-done | bytes 278552
  33.9 0.6 norm.1
  34.5 4.4 %collective-permute-start = (bf16[2,256,128]{2,1,0:T(8,128)(2,1)S(1)}, bf16[2,256,128]{2,1,0:T(8,128)(2,1)S(1)}, u32[]{:S(2)}, u32[]{:S(2)}) collective-permute-start(bf16[2,256,128]{2,1,0:T(8,128)(2,1)S(1)} %get-tuple-element.21.refs_0_), channel_id=1, source_target_pairs={{0,2},{1,3},{2,0},{3,1},{4,6},{5,7},{6,4},{7,5},{8,10},{9,11},{10,... | collective-permute-start | bytes 393224 | tf_op jit(solution)/shard_map/ppermute | solution.py:302
  38.9 3.2 %collective-permute-start.1 = (bf16[2,256,128]{2,1,0:T(8,128)(2,1)S(1)}, bf16[2,256,128]{2,1,0:T(8,128)(2,1)S(1)}, u32[]{:S(2)}, u32[]{:S(2)}) collective-permute-start(bf16[2,256,128]{2,1,0:T(8,128)(2,1)S(1)} %get-tuple-element.21.refs_0_), channel_id=1, source_target_pairs={{0,3},{1,2},{2,1},{3,0},{4,7},{5,6},{6,5},{7,4},{8,11},{9,10},{10,... | collective-permute-start | bytes 393224 | tf_op jit(solution)/shard_map/ppermute | solution.py:302
  42.1 7.1 %all-to-all-start.1 = ((f32[8,2,128]{2,1,0:T(2,128)}), f32[8,2,128]{2,1,0:T(2,128)S(1)}, u32[]{:S(2)}, u32[]{:S(2)}) async-start(f32[8,2,128]{2,1,0:T(2,128)} %get-tuple-element.19), calls=%async_computation.1 | async-start | bytes 16384 | tf_op jit(solution)/shard_map/all_to_all | solution.py:301
  49.3 1.9 %collective-permute-start.2 = (bf16[2,256,128]{2,1,0:T(8,128)(2,1)S(1)}, bf16[2,256,128]{2,1,0:T(8,128)(2,1)S(1)}, u32[]{:S(2)}, u32[]{:S(2)}) collective-permute-start(bf16[2,256,128]{2,1,0:T(8,128)(2,1)S(1)} %get-tuple-element.21.refs_0_), channel_id=1, source_target_pairs={{0,1},{1,0},{2,3},{3,2},{4,5},{5,4},{6,7},{7,6},{8,9},{9,8},{10,11... | collective-permute-start | bytes 393224 | tf_op jit(solution)/shard_map/ppermute | solution.py:302
  51.2 5.9 %all-to-all-done.1.sums = f32[8,2,128]{2,1,0:T(2,128)S(1)} async-done(((f32[8,2,128]{2,1,0:T(2,128)}), f32[8,2,128]{2,1,0:T(2,128)S(1)}, u32[]{:S(2)}, u32[]{:S(2)}) %all-to-all-start.1) | async-done | bytes 8224 | tf_op jit(solution)/shard_map/all_to_all | solution.py:301
  57.1 0.3 coef.1.normed
  57.4 0.0 collective-permute-done.refs_0_
  57.4 0.0 collective-permute-done.1.refs_1_
  57.4 0.9 %all-gather.3.cloned.1.call-done = bf16[16,512,128]{2,1,0:T(8,128)(2,1)} async-done(((bf16[2,512,128]{2,1,0:T(8,128)(2,1)}), bf16[16,512,128]{2,1,0:T(8,128)(2,1)}) %all-gather.3.cloned.1.call-update) | async-done | bytes 2097168 | tf_op jit(solution)/shard_map/all_gather | solution.py:288
  58.4 0.0 copy-start
  58.4 1.6 %copy-done = bf16[16,512,128]{2,1,0:T(8,128)(2,1)S(1)} copy-done((bf16[16,512,128]{2,1,0:T(8,128)(2,1)S(1)}, bf16[16,512,128]{2,1,0:T(8,128)(2,1)}, u32[]{:S(2)}) %copy-start) | copy-done | bytes 2097176
  60.0 0.0 copy-start.1
  60.0 1.9 %attend23.1 = (bf16[544,128]{1,0:T(8,128)(2,1)S(1)}, bf16[544,128]{1,0:T(8,128)(2,1)S(1)}, bf16[8,2,256,128]{3,2,1,0:T(8,128)(2,1)S(1)}) custom-call(bf16[8,2,512,128]{3,2,1,0:T(8,128)(2,1)S(1)} %bitcast.11, f32[2,8,2,128,128]{4,3,2,1,0:T(8,128)S(1)} %coef.1.normed, bf16[2,256,128]{2,1,0:T(8,128)(2,1)S(1)} %collective-permute-done.refs_0_, ...), custom_call_target="tpu_custom_call" | custom-call | flops 805306368 | bytes 4000000 | tf_op jit(solution)/shard_map/attend23/pallas_call | solution.py:315
  61.9 4.6 %collective-permute-start.4 = (bf16[544,128]{1,0:T(8,128)(2,1)S(1)}, bf16[544,128]{1,0:T(8,128)(2,1)S(1)}, u32[]{:S(2)}, u32[]{:S(2)}) collective-permute-start(bf16[544,128]{1,0:T(8,128)(2,1)S(1)} %get-tuple-element.28), channel_id=1, source_target_pairs={{0,2},{1,3},{2,0},{3,1},{4,6},{5,7},{6,4},{7,5},{8,10},{9,11},{10,... | collective-permute-start | bytes 417800 | tf_op jit(solution)/shard_map/ppermute | solution.py:302
  66.5 3.1 %collective-permute-start.5 = (bf16[544,128]{1,0:T(8,128)(2,1)S(1)}, bf16[544,128]{1,0:T(8,128)(2,1)S(1)}, u32[]{:S(2)}, u32[]{:S(2)}) collective-permute-start(bf16[544,128]{1,0:T(8,128)(2,1)S(1)} %get-tuple-element.29), channel_id=1, source_target_pairs={{0,3},{1,2},{2,1},{3,0},{4,7},{5,6},{6,5},{7,4},{8,11},{9,10},{10,... | collective-permute-start | bytes 417800 | tf_op jit(solution)/shard_map/ppermute | solution.py:302
  69.6 0.0 collective-permute-done.2.refs_0_
  69.6 0.0 copy-done.1
  69.6 1.4 %attend1.1 = bf16[528,128]{1,0:T(8,128)(2,1)S(1)} custom-call(bf16[8,2,512,128]{3,2,1,0:T(8,128)(2,1)S(1)} %bitcast.12, bf16[8,2,256,128]{3,2,1,0:T(8,128)(2,1)S(1)} %get-tuple-element.25.normed, bf16[2,256,128]{2,1,0:T(8,128)(2,1)S(1)} %collective-permute-done.2.refs_0_), custom_call_target="tpu_custom_call" | custom-call | flops 402653184 | bytes 4000000 | tf_op jit(solution)/shard_map/attend1/pallas_call | solution.py:315
  71.0 2.4 %collective-permute-start.3 = (bf16[528,128]{1,0:T(8,128)(2,1)S(1)}, bf16[528,128]{1,0:T(8,128)(2,1)S(1)}, u32[]{:S(2)}, u32[]{:S(2)}) collective-permute-start(bf16[528,128]{1,0:T(8,128)(2,1)S(1)} %attend1.1), channel_id=1, source_target_pairs={{0,1},{1,0},{2,3},{3,2},{4,5},{5,4},{6,7},{7,6},{8,9},{9,8},{10,11... | collective-permute-start | bytes 405512 | tf_op jit(solution)/shard_map/ppermute | solution.py:302
  73.5 1.4 %attend0.1.p0 = bf16[528,128]{1,0:T(8,128)(2,1)S(1)} custom-call(bf16[8,2,512,128]{3,2,1,0:T(8,128)(2,1)S(1)} %bitcast.13, bf16[8,2,256,128]{3,2,1,0:T(8,128)(2,1)S(1)} %get-tuple-element.25.normed, bf16[2,256,128]{2,1,0:T(8,128)(2,1)S(1)} %get-tuple-element.21.refs_0_), custom_call_target="tpu_custom_call" | custom-call | flops 402653184 | bytes 4000000 | tf_op jit(solution)/shard_map/attend0/pallas_call | solution.py:315
  74.9 3.1 %collective-permute-done.3.p1 = bf16[528,128]{1,0:T(8,128)(2,1)S(1)} collective-permute-done((bf16[528,128]{1,0:T(8,128)(2,1)S(1)}, bf16[528,128]{1,0:T(8,128)(2,1)S(1)}, u32[]{:S(2)}, u32[]{:S(2)}) %collective-permute-start.3) | collective-permute-done | bytes 135200 | tf_op jit(solution)/shard_map/ppermute | solution.py:302
  78.0 0.0 collective-permute-done.4.p2
  78.0 0.0 collective-permute-done.5.p3
  78.0 0.9 %merge.1 = (bf16[256,128]{1,0:T(8,128)(2,1)}, bf16[256,128]{1,0:T(8,128)(2,1)}) custom-call(bf16[528,128]{1,0:T(8,128)(2,1)S(1)} %attend0.1.p0, bf16[528,128]{1,0:T(8,128)(2,1)S(1)} %collective-permute-done.3.p1, bf16[544,128]{1,0:T(8,128)(2,1)S(1)} %collective-permute-done.4.p2, bf16[544,128]{1,0:T(8,128)(2,1)S(1)} %collective-permute-done.5.p3), custom_call_target="tpu_custom_call" | custom-call | flops 1 | bytes 1 | tf_op jit(solution)/shard_map/merge/pallas_call | solution.py:333
Async XLA Ops:
  7.2 51.2 %all-gather.3.cloned.1.call-start = ((), (), s32[]{:S(2)}) async-start(), calls=%async_computation.2 | async-start | bytes 2359296 | tf_op jit(solution)/shard_map/all_gather | solution.py:288
  32.9 1.0 %copy-start.2 = (f32[2,2,136,128]{3,2,1,0:T(8,128)S(1)}, f32[2,2,136,128]{3,2,1,0:T(8,128)}, u32[]{:S(2)}) copy-start(f32[2,2,136,128]{3,2,1,0:T(8,128)} %get-tuple-element.18.scaled) | copy-start | bytes 835588
  34.5 22.9 %collective-permute-start = (bf16[2,256,128]{2,1,0:T(8,128)(2,1)S(1)}, bf16[2,256,128]{2,1,0:T(8,128)(2,1)S(1)}, u32[]{:S(2)}, u32[]{:S(2)}) collective-permute-start(bf16[2,256,128]{2,1,0:T(8,128)(2,1)S(1)} %get-tuple-element.21.refs_0_), channel_id=1, source_target_pairs={{0,2},{1,3},{2,0},{3,1},{4,6},{5,7},{6,4},{7,5},{8,10},{9,11},{10,... | collective-permute-start | bytes 393224 | tf_op jit(solution)/shard_map/ppermute | solution.py:302
  38.9 18.5 %collective-permute-start.1 = (bf16[2,256,128]{2,1,0:T(8,128)(2,1)S(1)}, bf16[2,256,128]{2,1,0:T(8,128)(2,1)S(1)}, u32[]{:S(2)}, u32[]{:S(2)}) collective-permute-start(bf16[2,256,128]{2,1,0:T(8,128)(2,1)S(1)} %get-tuple-element.21.refs_0_), channel_id=1, source_target_pairs={{0,3},{1,2},{2,1},{3,0},{4,7},{5,6},{6,5},{7,4},{8,11},{9,10},{10,... | collective-permute-start | bytes 393224 | tf_op jit(solution)/shard_map/ppermute | solution.py:302
  42.1 14.9 %all-to-all-start.1 = ((f32[8,2,128]{2,1,0:T(2,128)}), f32[8,2,128]{2,1,0:T(2,128)S(1)}, u32[]{:S(2)}, u32[]{:S(2)}) async-start(f32[8,2,128]{2,1,0:T(2,128)} %get-tuple-element.19), calls=%async_computation.1 | async-start | bytes 16384 | tf_op jit(solution)/shard_map/all_to_all | solution.py:301
  49.3 20.4 %collective-permute-start.2 = (bf16[2,256,128]{2,1,0:T(8,128)(2,1)S(1)}, bf16[2,256,128]{2,1,0:T(8,128)(2,1)S(1)}, u32[]{:S(2)}, u32[]{:S(2)}) collective-permute-start(bf16[2,256,128]{2,1,0:T(8,128)(2,1)S(1)} %get-tuple-element.21.refs_0_), channel_id=1, source_target_pairs={{0,1},{1,0},{2,3},{3,2},{4,5},{5,4},{6,7},{7,6},{8,9},{9,8},{10,11... | collective-permute-start | bytes 393224 | tf_op jit(solution)/shard_map/ppermute | solution.py:302
  58.4 1.6 %copy-start = (bf16[16,512,128]{2,1,0:T(8,128)(2,1)S(1)}, bf16[16,512,128]{2,1,0:T(8,128)(2,1)}, u32[]{:S(2)}) copy-start(bf16[16,512,128]{2,1,0:T(8,128)(2,1)} %all-gather.3.cloned.1.call-done) | copy-start | bytes 6291460
  60.0 9.7 %copy-start.1 = (bf16[16,512,128]{2,1,0:T(8,128)(2,1)S(1)}, bf16[16,512,128]{2,1,0:T(8,128)(2,1)}, u32[]{:S(2)}) copy-start(bf16[16,512,128]{2,1,0:T(8,128)(2,1)} %all-gather.3.cloned.1.call-done) | copy-start | bytes 6291460
  61.9 16.0 %collective-permute-start.4 = (bf16[544,128]{1,0:T(8,128)(2,1)S(1)}, bf16[544,128]{1,0:T(8,128)(2,1)S(1)}, u32[]{:S(2)}, u32[]{:S(2)}) collective-permute-start(bf16[544,128]{1,0:T(8,128)(2,1)S(1)} %get-tuple-element.28), channel_id=1, source_target_pairs={{0,2},{1,3},{2,0},{3,1},{4,6},{5,7},{6,4},{7,5},{8,10},{9,11},{10,... | collective-permute-start | bytes 417800 | tf_op jit(solution)/shard_map/ppermute | solution.py:302
  66.5 11.4 %collective-permute-start.5 = (bf16[544,128]{1,0:T(8,128)(2,1)S(1)}, bf16[544,128]{1,0:T(8,128)(2,1)S(1)}, u32[]{:S(2)}, u32[]{:S(2)}) collective-permute-start(bf16[544,128]{1,0:T(8,128)(2,1)S(1)} %get-tuple-element.29), channel_id=1, source_target_pairs={{0,3},{1,2},{2,1},{3,0},{4,7},{5,6},{6,5},{7,4},{8,11},{9,10},{10,... | collective-permute-start | bytes 417800 | tf_op jit(solution)/shard_map/ppermute | solution.py:302
  71.0 6.9 %collective-permute-start.3 = (bf16[528,128]{1,0:T(8,128)(2,1)S(1)}, bf16[528,128]{1,0:T(8,128)(2,1)S(1)}, u32[]{:S(2)}, u32[]{:S(2)}) collective-permute-start(bf16[528,128]{1,0:T(8,128)(2,1)S(1)} %attend1.1), channel_id=1, source_target_pairs={{0,1},{1,0},{2,3},{3,2},{4,5},{5,4},{6,7},{7,6},{8,9},{9,8},{10,11... | collective-permute-start | bytes 405512 | tf_op jit(solution)/shard_map/ppermute | solution.py:302
Sparse Core Ops, SparseCore 0:
  10.1 48.2 all-gather.2

commit v2 on v1

--- a/solution.py
+++ b/solution.py
@@ -85,8 +85,9 @@
 
 def bulk_kernel(k, tk, v, tv, out, raw, wide, packed, sems):
     heads = loader((k, tk, v, tv), raw, wide, sems)
-    for i in range(4):
-        for h, block in enumerate(heads(i)):
+    pairs = [heads(i) for i in range(4)]
+    for i, pair in enumerate(pairs):
+        for h, block in enumerate(pair):
             block = block if i < 2 else block.T
             packed[h, i * 128 : (i + 1) * 128] = block.astype(jnp.bfloat16)
     send = pltpu.make_async_copy(packed, out, sems.at[4])
@@ -216,27 +217,47 @@
             ref[PART:] = jnp.zeros((ref.shape[0] - PART, HS), bf16)
 
 
-def merge_kernel(p0, p1, p2, p3, out_ref, tan_ref, wide):
-    f32, bf16 = jnp.float32, jnp.bfloat16
+def statistics(part, h):
+    rows = part[512:528].astype(jnp.float32)[6 * h : 6 * h + 6]
+    return rows[0:1] + rows[1:2] + rows[2:3], rows[3:4] + rows[4:5] + rows[5:6]
+
+
+def three_kernel(p0, p2, p3, sum_out, stat_out):
+    f32 = jnp.float32
     for h in range(LOCAL):
-        parts = (p0, p1, p2, p3)
-        logs, means = [], []
-        for z in range(Z):
-            stats = parts[z][512:528].astype(f32)[6 * h : 6 * h + 6]
-            logs.append(stats[0:1] + stats[1:2] + stats[2:3])
-            means.append(stats[3:4] + stats[4:5] + stats[5:6])
-        top = jnp.maximum(jnp.maximum(logs[0], logs[1]), jnp.maximum(logs[2], logs[3]))
+        logs, means = zip(*[statistics(part, h) for part in (p0, p2, p3)])
+        top = jnp.maximum(jnp.maximum(logs[0], logs[1]), logs[2])
         weights = [jnp.exp2(x - top) for x in logs]
-        inverse = 1.0 / (weights[0] + weights[1] + weights[2] + weights[3])
+        total = weights[0] + weights[1] + weights[2]
+        inverse = 1.0 / total
         weights = [w * inverse for w in weights]
         mean = sum(w * m for w, m in zip(weights, means))
         out = jnp.zeros((HS, ROWS), f32)
         tangent = jnp.zeros((HS, ROWS), f32)
-        for z in range(Z):
-            piece = parts[z][h * 256 : h * 256 + 128].astype(f32)
-            out = out + weights[z] * piece
-            tangent = tangent + weights[z] * parts[z][h * 256 + 128 : h * 256 + 256].astype(f32)
-            tangent = tangent + (weights[z] * (means[z] - mean)) * piece
+        for part, weight, own_mean in zip((p0, p2, p3), weights, means):
+            piece = part[h * 256 : h * 256 + 128].astype(f32)
+            out = out + weight * piece
+            tangent = tangent + weight * part[h * 256 + 128 : h * 256 + 256].astype(f32)
+            tangent = tangent + (weight * (own_mean - mean)) * piece
+        sum_out[h, 0], sum_out[h, 1] = out, tangent
+        stat_out[h, 0] = jnp.broadcast_to(top + jnp.log2(total), (8, ROWS))
+        stat_out[h, 1] = jnp.broadcast_to(mean, (8, ROWS))
+
+
+def merge_kernel(sums, stats, last, out_ref, tan_ref, wide):
+    f32, bf16 = jnp.float32, jnp.bfloat16
+    for h in range(LOCAL):
+        log, mean = stats[h, 0, 0:1], stats[h, 1, 0:1]
+        last_log, last_mean = statistics(last, h)
+        top = jnp.maximum(log, last_log)
+        weight, last_weight = jnp.exp2(log - top), jnp.exp2(last_log - top)
+        inverse = 1.0 / (weight + last_weight)
+        weight, last_weight = weight * inverse, last_weight * inverse
+        piece = last[h * 256 : h * 256 + 128].astype(f32)
+        tan_piece = last[h * 256 + 128 : h * 256 + 256].astype(f32)
+        out = weight * sums[h, 0] + last_weight * piece
+        tangent = weight * sums[h, 1] + last_weight * tan_piece
+        tangent = tangent + (weight * last_weight * (mean - last_mean)) * (sums[h, 0] - piece)
         wide[0, pl.ds(h, ROWS, stride=LOCAL), :] = out.T
         wide[1, pl.ds(h, ROWS, stride=LOCAL), :] = tangent.T
     out_ref[...] = wide[0].astype(bf16)
@@ -329,7 +350,14 @@
     (part1,) = attend(bulk, normed, 1)
     bulk, part1 = lax.optimization_barrier((bulk, part1))
     (part0,) = attend(bulk, normed, 0)
-    parts = [part0, trade(part1, 1), trade(part2, 2), trade(part3, 3)]
+    last = trade(part1, 1)
+    sums, stats = pl.pallas_call(
+        three_kernel,
+        out_shape=(struct((LOCAL, 2, HS, ROWS), f32), struct((LOCAL, 2, 8, ROWS), f32)),
+        compiler_params=params(),
+        cost_estimate=SMALL,
+        name="three",
+    )(part0, trade(part2, 2), trade(part3, 3))
     out, tangent = pl.pallas_call(
         merge_kernel,
         out_shape=(struct((ROWS * LOCAL, HS), bf16),) * 2,
@@ -337,7 +365,7 @@
         compiler_params=params(),
         cost_estimate=SMALL,
         name="merge",
-    )(*parts)
+    )(sums, stats, last)
     shape = queries.shape
     return (out.reshape(shape), tangent.reshape(shape))
 

time: 86.3 us -> 86.2 us (level)
  transfers between devices with their start and end apart: 8 -> 8, of which waited for: 3 -> 4; matrix products, arithmetic and copies ran while one was open for 0% -> 0% of each run, Pallas kernels for 9% -> 9%
where the time goes in v2:
time: 86.2 us; the launch traced here: 85.7 us
  starting transfers between devices  26.9 us (31%)
  blocking collectives  21.9 us (25%)
  between operations  14.2 us (16%)
  Pallas kernels  10.3 us (12%)
  waiting for transfers between devices  9.85 us (11%)
  local copies, waits for them, and re-layouts  2.55 us (3%)
    all_to_all x1, blocking collectives, shards(): stats = lax.all_to_all(stats, 'dp', 0, 0)  21.9 us
    ppermute x6, starting transfers between devices, shards(): trade = lambda x, i: lax.ppermute(x, 'seq', swaps(Y * Z, i))  19.8 us
    all_to_all x1, starting transfers between devices, shards(): sums = lax.all_to_all(sums, 'seq', 0, 0, axis_index_groups=Y_GROUPS)  7.11 us
    all_to_all x1, waiting for transfers between devices, shards(): sums = lax.all_to_all(sums, 'seq', 0, 0, axis_index_groups=Y_GROUPS)  5.88 us
    pallas_call x3, Pallas kernels, attend(): pl.pallas_call(functools.partial(attend_kernel, count), out_shape=(struct...  4.72 us
    ppermute x6, waiting for transfers between devices, shards(): trade = lambda x, i: lax.ppermute(x, 'seq', swaps(Y * Z, i))  3 us
    unnamed x6, local copies, waits for them, and re-layouts  2.55 us
    pallas_call x1, Pallas kernels, shards(): pl.pallas_call(stats_kernel, out_shape=(struct((DP, 4, ROWS), f32), struc...  1.83 us
  transfers between devices with their start and end apart: 8, of which 4 were waited for; matrix products, arithmetic and copies ran while one was open for 0% of the time, Pallas kernels for 9%

profile of v2, /device:TPU:2, one launch (start us, length us, event | category | flops | bytes accessed | tf_op | source)
XLA Modules:
  0.0 85.7 jit_solution(2018861887274583471)
XLA Ops:
  7.2 0.0 all-gather.3.cloned.1.call-start
  7.2 1.8 %bulk.1 = bf16[2,512,128]{2,1,0:T(8,128)(2,1)} custom-call(bf16[256,128]{1,0:T(8,128)(2,1)} %bitcast.14, bf16[256,128]{1,0:T(8,128)(2,1)} %bitcast.16, bf16[256,128]{1,0:T(8,128)(2,1)} %bitcast.20, bf16[256,128]{1,0:T(8,128)(2,1)} %bitcast.21), custom_call_target="tpu_custom_call" | custom-call | flops 1 | bytes 1 | tf_op jit(solution)/shard_map/bulk/pallas_call | solution.py:294
  9.0 0.0 all-gather.3.cloned.1.call-update
  9.0 1.8 %stats.1 = (f32[16,4,128]{2,1,0:T(4,128)}, f32[2,2,136,128]{3,2,1,0:T(8,128)}) custom-call(bf16[256,128]{1,0:T(8,128)(2,1)} %bitcast.18, bf16[256,128]{1,0:T(8,128)(2,1)} %bitcast.15, bf16[256,128]{1,0:T(8,128)(2,1)} %bitcast.19, bf16[256,128]{1,0:T(8,128)(2,1)} %bitcast.17, f32[2,128]{1,0:T(2,128)} %bitcast.22, f32[2,128]{1,0:T(2,128)} %bitcast.23), custom_call_target="tpu_custom_call" | custom-call | flops 1 | bytes 1 | tf_op jit(solution)/shard_map/stats/pallas_call | solution.py:279
  10.9 21.9 %all_to_all.10.parts = f32[16,4,128]{2,1,0:T(4,128)S(1)} all-to-all(f32[16,4,128]{2,1,0:T(4,128)} %get-tuple-element.19), channel_id=1, replica_groups=mesh['dp'=16,'seq'=32] {'dp'}, dimensions={0} | all-to-all | bytes 65536 | tf_op jit(solution)/shard_map/all_to_all | solution.py:310
  32.8 0.0 copy-start.2
  32.8 1.0 %copy-done.2 = f32[2,2,136,128]{3,2,1,0:T(8,128)S(1)} copy-done((f32[2,2,136,128]{3,2,1,0:T(8,128)S(1)}, f32[2,2,136,128]{3,2,1,0:T(8,128)}, u32[]{:S(2)}) %copy-start.2) | copy-done | bytes 278552
  33.8 0.6 norm.1
  34.4 4.4 %collective-permute-start = (bf16[2,256,128]{2,1,0:T(8,128)(2,1)S(1)}, bf16[2,256,128]{2,1,0:T(8,128)(2,1)S(1)}, u32[]{:S(2)}, u32[]{:S(2)}) collective-permute-start(bf16[2,256,128]{2,1,0:T(8,128)(2,1)S(1)} %get-tuple-element.23.refs_0_), channel_id=1, source_target_pairs={{0,2},{1,3},{2,0},{3,1},{4,6},{5,7},{6,4},{7,5},{8,10},{9,11},{10,... | collective-permute-start | bytes 393224 | tf_op jit(solution)/shard_map/ppermute | solution.py:323
  38.8 3.2 %collective-permute-start.1 = (bf16[2,256,128]{2,1,0:T(8,128)(2,1)S(1)}, bf16[2,256,128]{2,1,0:T(8,128)(2,1)S(1)}, u32[]{:S(2)}, u32[]{:S(2)}) collective-permute-start(bf16[2,256,128]{2,1,0:T(8,128)(2,1)S(1)} %get-tuple-element.23.refs_0_), channel_id=1, source_target_pairs={{0,3},{1,2},{2,1},{3,0},{4,7},{5,6},{6,5},{7,4},{8,11},{9,10},{10,... | collective-permute-start | bytes 393224 | tf_op jit(solution)/shard_map/ppermute | solution.py:323
  42.0 7.1 %all-to-all-start.1 = ((f32[8,2,128]{2,1,0:T(2,128)}), f32[8,2,128]{2,1,0:T(2,128)S(1)}, u32[]{:S(2)}, u32[]{:S(2)}) async-start(f32[8,2,128]{2,1,0:T(2,128)} %get-tuple-element.21), calls=%async_computation.1 | async-start | bytes 16384 | tf_op jit(solution)/shard_map/all_to_all | solution.py:322
  49.2 1.9 %collective-permute-start.2 = (bf16[2,256,128]{2,1,0:T(8,128)(2,1)S(1)}, bf16[2,256,128]{2,1,0:T(8,128)(2,1)S(1)}, u32[]{:S(2)}, u32[]{:S(2)}) collective-permute-start(bf16[2,256,128]{2,1,0:T(8,128)(2,1)S(1)} %get-tuple-element.23.refs_0_), channel_id=1, source_target_pairs={{0,1},{1,0},{2,3},{3,2},{4,5},{5,4},{6,7},{7,6},{8,9},{9,8},{10,11... | collective-permute-start | bytes 393224 | tf_op jit(solution)/shard_map/ppermute | solution.py:323
  51.1 5.9 %all-to-all-done.1.sums = f32[8,2,128]{2,1,0:T(2,128)S(1)} async-done(((f32[8,2,128]{2,1,0:T(2,128)}), f32[8,2,128]{2,1,0:T(2,128)S(1)}, u32[]{:S(2)}, u32[]{:S(2)}) %all-to-all-start.1) | async-done | bytes 8224 | tf_op jit(solution)/shard_map/all_to_all | solution.py:322
  57.0 0.3 coef.1.normed
  57.3 0.0 collective-permute-done.refs_0_
  57.3 0.0 collective-permute-done.1.refs_1_
  57.3 1.0 %all-gather.3.cloned.1.call-done = bf16[16,512,128]{2,1,0:T(8,128)(2,1)} async-done(((bf16[2,512,128]{2,1,0:T(8,128)(2,1)}), bf16[16,512,128]{2,1,0:T(8,128)(2,1)}) %all-gather.3.cloned.1.call-update) | async-done | bytes 2097168 | tf_op jit(solution)/shard_map/all_gather | solution.py:309
  58.3 0.0 copy-start
  58.3 1.6 %copy-done = bf16[16,512,128]{2,1,0:T(8,128)(2,1)S(1)} copy-done((bf16[16,512,128]{2,1,0:T(8,128)(2,1)S(1)}, bf16[16,512,128]{2,1,0:T(8,128)(2,1)}, u32[]{:S(2)}) %copy-start) | copy-done | bytes 2097176
  59.9 0.0 copy-start.1
  59.9 1.9 %attend23.1 = (bf16[544,128]{1,0:T(8,128)(2,1)S(1)}, bf16[544,128]{1,0:T(8,128)(2,1)S(1)}, bf16[8,2,256,128]{3,2,1,0:T(8,128)(2,1)S(1)}) custom-call(bf16[8,2,512,128]{3,2,1,0:T(8,128)(2,1)S(1)} %bitcast.11, f32[2,8,2,128,128]{4,3,2,1,0:T(8,128)S(1)} %coef.1.normed, bf16[2,256,128]{2,1,0:T(8,128)(2,1)S(1)} %collective-permute-done.refs_0_, ...), custom_call_target="tpu_custom_call" | custom-call | flops 805306368 | bytes 4000000 | tf_op jit(solution)/shard_map/attend23/pallas_call | solution.py:336
  61.8 4.7 %collective-permute-start.3 = (bf16[544,128]{1,0:T(8,128)(2,1)S(1)}, bf16[544,128]{1,0:T(8,128)(2,1)S(1)}, u32[]{:S(2)}, u32[]{:S(2)}) collective-permute-start(bf16[544,128]{1,0:T(8,128)(2,1)S(1)} %get-tuple-element.29), channel_id=1, source_target_pairs={{0,2},{1,3},{2,0},{3,1},{4,6},{5,7},{6,4},{7,5},{8,10},{9,11},{10,... | collective-permute-start | bytes 417800 | tf_op jit(solution)/shard_map/ppermute | solution.py:323
  66.6 3.1 %collective-permute-start.4 = (bf16[544,128]{1,0:T(8,128)(2,1)S(1)}, bf16[544,128]{1,0:T(8,128)(2,1)S(1)}, u32[]{:S(2)}, u32[]{:S(2)}) collective-permute-start(bf16[544,128]{1,0:T(8,128)(2,1)S(1)} %get-tuple-element.30), channel_id=1, source_target_pairs={{0,3},{1,2},{2,1},{3,0},{4,7},{5,6},{6,5},{7,4},{8,11},{9,10},{10,... | collective-permute-start | bytes 417800 | tf_op jit(solution)/shard_map/ppermute | solution.py:323
  69.7 0.0 collective-permute-done.2.refs_0_
  69.7 0.0 copy-done.1
  69.7 1.4 %attend1.1 = bf16[528,128]{1,0:T(8,128)(2,1)S(1)} custom-call(bf16[8,2,512,128]{3,2,1,0:T(8,128)(2,1)S(1)} %bitcast.12, bf16[8,2,256,128]{3,2,1,0:T(8,128)(2,1)S(1)} %get-tuple-element.27.normed, bf16[2,256,128]{2,1,0:T(8,128)(2,1)S(1)} %collective-permute-done.2.refs_0_), custom_call_target="tpu_custom_call" | custom-call | flops 402653184 | bytes 4000000 | tf_op jit(solution)/shard_map/attend1/pallas_call | solution.py:336
  71.1 2.3 %collective-permute-start.5 = (bf16[528,128]{1,0:T(8,128)(2,1)S(1)}, bf16[528,128]{1,0:T(8,128)(2,1)S(1)}, u32[]{:S(2)}, u32[]{:S(2)}) collective-permute-start(bf16[528,128]{1,0:T(8,128)(2,1)S(1)} %attend1.1), channel_id=1, source_target_pairs={{0,1},{1,0},{2,3},{3,2},{4,5},{5,4},{6,7},{7,6},{8,9},{9,8},{10,11... | collective-permute-start | bytes 405512 | tf_op jit(solution)/shard_map/ppermute | solution.py:323
  73.5 1.4 %attend0.1.p0 = bf16[528,128]{1,0:T(8,128)(2,1)S(1)} custom-call(bf16[8,2,512,128]{3,2,1,0:T(8,128)(2,1)S(1)} %bitcast.13, bf16[8,2,256,128]{3,2,1,0:T(8,128)(2,1)S(1)} %get-tuple-element.27.normed, bf16[2,256,128]{2,1,0:T(8,128)(2,1)S(1)} %get-tuple-element.23.refs_0_), custom_call_target="tpu_custom_call" | custom-call | flops 402653184 | bytes 4000000 | tf_op jit(solution)/shard_map/attend0/pallas_call | solution.py:336
  74.9 0.0 collective-permute-done.3.p2
  74.9 0.7 collective-permute-done.4.p3
  75.6 0.2 three.1
  75.7 2.3 %collective-permute-done.5.last = bf16[528,128]{1,0:T(8,128)(2,1)S(1)} collective-permute-done((bf16[528,128]{1,0:T(8,128)(2,1)S(1)}, bf16[528,128]{1,0:T(8,128)(2,1)S(1)}, u32[]{:S(2)}, u32[]{:S(2)}) %collective-permute-start.5) | collective-permute-done | bytes 135200 | tf_op jit(solution)/shard_map/ppermute | solution.py:323
  78.0 0.8 merge.1
Async XLA Ops:
  7.2 51.1 %all-gather.3.cloned.1.call-start = ((), (), s32[]{:S(2)}) async-start(), calls=%async_computation.2 | async-start | bytes 2359296 | tf_op jit(solution)/shard_map/all_gather | solution.py:309
  32.8 1.0 %copy-start.2 = (f32[2,2,136,128]{3,2,1,0:T(8,128)S(1)}, f32[2,2,136,128]{3,2,1,0:T(8,128)}, u32[]{:S(2)}) copy-start(f32[2,2,136,128]{3,2,1,0:T(8,128)} %get-tuple-element.20.scaled) | copy-start | bytes 835588
  34.4 22.9 %collective-permute-start = (bf16[2,256,128]{2,1,0:T(8,128)(2,1)S(1)}, bf16[2,256,128]{2,1,0:T(8,128)(2,1)S(1)}, u32[]{:S(2)}, u32[]{:S(2)}) collective-permute-start(bf16[2,256,128]{2,1,0:T(8,128)(2,1)S(1)} %get-tuple-element.23.refs_0_), channel_id=1, source_target_pairs={{0,2},{1,3},{2,0},{3,1},{4,6},{5,7},{6,4},{7,5},{8,10},{9,11},{10,... | collective-permute-start | bytes 393224 | tf_op jit(solution)/shard_map/ppermute | solution.py:323
  38.8 18.5 %collective-permute-start.1 = (bf16[2,256,128]{2,1,0:T(8,128)(2,1)S(1)}, bf16[2,256,128]{2,1,0:T(8,128)(2,1)S(1)}, u32[]{:S(2)}, u32[]{:S(2)}) collective-permute-start(bf16[2,256,128]{2,1,0:T(8,128)(2,1)S(1)} %get-tuple-element.23.refs_0_), channel_id=1, source_target_pairs={{0,3},{1,2},{2,1},{3,0},{4,7},{5,6},{6,5},{7,4},{8,11},{9,10},{10,... | collective-permute-start | bytes 393224 | tf_op jit(solution)/shard_map/ppermute | solution.py:323
  42.0 14.9 %all-to-all-start.1 = ((f32[8,2,128]{2,1,0:T(2,128)}), f32[8,2,128]{2,1,0:T(2,128)S(1)}, u32[]{:S(2)}, u32[]{:S(2)}) async-start(f32[8,2,128]{2,1,0:T(2,128)} %get-tuple-element.21), calls=%async_computation.1 | async-start | bytes 16384 | tf_op jit(solution)/shard_map/all_to_all | solution.py:322
  49.2 20.5 %collective-permute-start.2 = (bf16[2,256,128]{2,1,0:T(8,128)(2,1)S(1)}, bf16[2,256,128]{2,1,0:T(8,128)(2,1)S(1)}, u32[]{:S(2)}, u32[]{:S(2)}) collective-permute-start(bf16[2,256,128]{2,1,0:T(8,128)(2,1)S(1)} %get-tuple-element.23.refs_0_), channel_id=1, source_target_pairs={{0,1},{1,0},{2,3},{3,2},{4,5},{5,4},{6,7},{7,6},{8,9},{9,8},{10,11... | collective-permute-start | bytes 393224 | tf_op jit(solution)/shard_map/ppermute | solution.py:323
  58.3 1.6 %copy-start = (bf16[16,512,128]{2,1,0:T(8,128)(2,1)S(1)}, bf16[16,512,128]{2,1,0:T(8,128)(2,1)}, u32[]{:S(2)}) copy-start(bf16[16,512,128]{2,1,0:T(8,128)(2,1)} %all-gather.3.cloned.1.call-done) | copy-start | bytes 6291460
  59.9 9.8 %copy-start.1 = (bf16[16,512,128]{2,1,0:T(8,128)(2,1)S(1)}, bf16[16,512,128]{2,1,0:T(8,128)(2,1)}, u32[]{:S(2)}) copy-start(bf16[16,512,128]{2,1,0:T(8,128)(2,1)} %all-gather.3.cloned.1.call-done) | copy-start | bytes 6291460
  61.8 13.0 %collective-permute-start.3 = (bf16[544,128]{1,0:T(8,128)(2,1)S(1)}, bf16[544,128]{1,0:T(8,128)(2,1)S(1)}, u32[]{:S(2)}, u32[]{:S(2)}) collective-permute-start(bf16[544,128]{1,0:T(8,128)(2,1)S(1)} %get-tuple-element.29), channel_id=1, source_target_pairs={{0,2},{1,3},{2,0},{3,1},{4,6},{5,7},{6,4},{7,5},{8,10},{9,11},{10,... | collective-permute-start | bytes 417800 | tf_op jit(solution)/shard_map/ppermute | solution.py:323
  66.6 9.0 %collective-permute-start.4 = (bf16[544,128]{1,0:T(8,128)(2,1)S(1)}, bf16[544,128]{1,0:T(8,128)(2,1)S(1)}, u32[]{:S(2)}, u32[]{:S(2)}) collective-permute-start(bf16[544,128]{1,0:T(8,128)(2,1)S(1)} %get-tuple-element.30), channel_id=1, source_target_pairs={{0,3},{1,2},{2,1},{3,0},{4,7},{5,6},{6,5},{7,4},{8,11},{9,10},{10,... | collective-permute-start | bytes 417800 | tf_op jit(solution)/shard_map/ppermute | solution.py:323
  71.1 6.9 %collective-permute-start.5 = (bf16[528,128]{1,0:T(8,128)(2,1)S(1)}, bf16[528,128]{1,0:T(8,128)(2,1)S(1)}, u32[]{:S(2)}, u32[]{:S(2)}) collective-permute-start(bf16[528,128]{1,0:T(8,128)(2,1)S(1)} %attend1.1), channel_id=1, source_target_pairs={{0,1},{1,0},{2,3},{3,2},{4,5},{5,4},{6,7},{7,6},{8,9},{9,8},{10,11... | collective-permute-start | bytes 405512 | tf_op jit(solution)/shard_map/ppermute | solution.py:323
Sparse Core Ops, SparseCore 0:
  10.1 48.1 all-gather.2

commit v3 on v2

--- a/solution.py
+++ b/solution.py
@@ -134,17 +134,17 @@
     queries, outs, (s_ref, t_ref) = refs[:count], refs[count : 2 * count], refs[-2:]
     if count > 1:
         coef, normed = normed, refs[2 * count]
-        for h in range(LOCAL):
+    nt = (((1,), (1,)), ((), ()))
+    cols = count * ROWS
+
+    rows = []
+    for h in range(LOCAL):
+        if count > 1:
             for y in range(Y):
                 key = bulk[y, h, 0:128].astype(f32)
                 tan_key = bulk[y, h, 128:256].astype(f32)
                 normed[y, h, 0:128] = (key * coef[0, y, h]).astype(bf16)
                 normed[y, h, 128:256] = (tan_key * coef[0, y, h] - key * coef[1, y, h]).astype(bf16)
-    nt = (((1,), (1,)), ((), ()))
-    cols = count * ROWS
-
-    rows = []
-    for h in range(LOCAL):
         query = jnp.concatenate([q[h, 0:128] for q in queries], axis=0)
         tan_query = jnp.concatenate([q[h, 128:256] for q in queries], axis=0)
         both = jnp.concatenate([tan_query, query], axis=1)

time: 86.2 us -> 86.2 us (level)
  no operation moved by 1% of the time
where the time goes in v3:
time: 86.2 us; the launch traced here: 85.7 us
  starting transfers between devices  26.9 us (31%)
  blocking collectives  21.9 us (25%)
  between operations  14.2 us (16%)
  Pallas kernels  10.3 us (12%)
  waiting for transfers between devices  9.85 us (11%)
  local copies, waits for them, and re-layouts  2.55 us (3%)
    all_to_all x1, blocking collectives, shards(): stats = lax.all_to_all(stats, 'dp', 0, 0)  21.9 us
    ppermute x6, starting transfers between devices, shards(): trade = lambda x, i: lax.ppermute(x, 'seq', swaps(Y * Z, i))  19.8 us
    all_to_all x1, starting transfers between devices, shards(): sums = lax.all_to_all(sums, 'seq', 0, 0, axis_index_groups=Y_GROUPS)  7.11 us
    all_to_all x1, waiting for transfers between devices, shards(): sums = lax.all_to_all(sums, 'seq', 0, 0, axis_index_groups=Y_GROUPS)  5.88 us
    pallas_call x3, Pallas kernels, attend(): pl.pallas_call(functools.partial(attend_kernel, count), out_shape=(struct...  4.72 us
    ppermute x6, waiting for transfers between devices, shards(): trade = lambda x, i: lax.ppermute(x, 'seq', swaps(Y * Z, i))  3 us
    unnamed x6, local copies, waits for them, and re-layouts  2.55 us
    pallas_call x1, Pallas kernels, shards(): pl.pallas_call(stats_kernel, out_shape=(struct((DP, 4, ROWS), f32), struc...  1.83 us
  transfers between devices with their start and end apart: 8, of which 4 were waited for; matrix products, arithmetic and copies ran while one was open for 0% of the time, Pallas kernels for 9%

profile of v3, /device:TPU:2, one launch (start us, length us, event | category | flops | bytes accessed | tf_op | source)
XLA Modules:
  0.0 85.7 jit_solution(2018861887274583471)
XLA Ops:
  7.2 0.0 all-gather.3.cloned.1.call-start
  7.2 1.8 %bulk.1 = bf16[2,512,128]{2,1,0:T(8,128)(2,1)} custom-call(bf16[256,128]{1,0:T(8,128)(2,1)} %bitcast.14, bf16[256,128]{1,0:T(8,128)(2,1)} %bitcast.16, bf16[256,128]{1,0:T(8,128)(2,1)} %bitcast.20, bf16[256,128]{1,0:T(8,128)(2,1)} %bitcast.21), custom_call_target="tpu_custom_call" | custom-call | flops 1 | bytes 1 | tf_op jit(solution)/shard_map/bulk/pallas_call | solution.py:294
  9.0 0.0 all-gather.3.cloned.1.call-update
  9.0 1.8 %stats.1 = (f32[16,4,128]{2,1,0:T(4,128)}, f32[2,2,136,128]{3,2,1,0:T(8,128)}) custom-call(bf16[256,128]{1,0:T(8,128)(2,1)} %bitcast.18, bf16[256,128]{1,0:T(8,128)(2,1)} %bitcast.15, bf16[256,128]{1,0:T(8,128)(2,1)} %bitcast.19, bf16[256,128]{1,0:T(8,128)(2,1)} %bitcast.17, f32[2,128]{1,0:T(2,128)} %bitcast.22, f32[2,128]{1,0:T(2,128)} %bitcast.23), custom_call_target="tpu_custom_call" | custom-call | flops 1 | bytes 1 | tf_op jit(solution)/shard_map/stats/pallas_call | solution.py:279
  10.9 21.9 %all_to_all.10.parts = f32[16,4,128]{2,1,0:T(4,128)S(1)} all-to-all(f32[16,4,128]{2,1,0:T(4,128)} %get-tuple-element.19), channel_id=1, replica_groups=mesh['dp'=16,'seq'=32] {'dp'}, dimensions={0} | all-to-all | bytes 65536 | tf_op jit(solution)/shard_map/all_to_all | solution.py:310
  32.8 0.0 copy-start.2
  32.8 1.0 %copy-done.2 = f32[2,2,136,128]{3,2,1,0:T(8,128)S(1)} copy-done((f32[2,2,136,128]{3,2,1,0:T(8,128)S(1)}, f32[2,2,136,128]{3,2,1,0:T(8,128)}, u32[]{:S(2)}) %copy-start.2) | copy-done | bytes 278552
  33.8 0.6 norm.1
  34.4 4.4 %collective-permute-start = (bf16[2,256,128]{2,1,0:T(8,128)(2,1)S(1)}, bf16[2,256,128]{2,1,0:T(8,128)(2,1)S(1)}, u32[]{:S(2)}, u32[]{:S(2)}) collective-permute-start(bf16[2,256,128]{2,1,0:T(8,128)(2,1)S(1)} %get-tuple-element.23.refs_0_), channel_id=1, source_target_pairs={{0,2},{1,3},{2,0},{3,1},{4,6},{5,7},{6,4},{7,5},{8,10},{9,11},{10,... | collective-permute-start | bytes 393224 | tf_op jit(solution)/shard_map/ppermute | solution.py:323
  38.8 3.2 %collective-permute-start.1 = (bf16[2,256,128]{2,1,0:T(8,128)(2,1)S(1)}, bf16[2,256,128]{2,1,0:T(8,128)(2,1)S(1)}, u32[]{:S(2)}, u32[]{:S(2)}) collective-permute-start(bf16[2,256,128]{2,1,0:T(8,128)(2,1)S(1)} %get-tuple-element.23.refs_0_), channel_id=1, source_target_pairs={{0,3},{1,2},{2,1},{3,0},{4,7},{5,6},{6,5},{7,4},{8,11},{9,10},{10,... | collective-permute-start | bytes 393224 | tf_op jit(solution)/shard_map/ppermute | solution.py:323
  42.0 7.1 %all-to-all-start.1 = ((f32[8,2,128]{2,1,0:T(2,128)}), f32[8,2,128]{2,1,0:T(2,128)S(1)}, u32[]{:S(2)}, u32[]{:S(2)}) async-start(f32[8,2,128]{2,1,0:T(2,128)} %get-tuple-element.21), calls=%async_computation.1 | async-start | bytes 16384 | tf_op jit(solution)/shard_map/all_to_all | solution.py:322
  49.2 1.9 %collective-permute-start.2 = (bf16[2,256,128]{2,1,0:T(8,128)(2,1)S(1)}, bf16[2,256,128]{2,1,0:T(8,128)(2,1)S(1)}, u32[]{:S(2)}, u32[]{:S(2)}) collective-permute-start(bf16[2,256,128]{2,1,0:T(8,128)(2,1)S(1)} %get-tuple-element.23.refs_0_), channel_id=1, source_target_pairs={{0,1},{1,0},{2,3},{3,2},{4,5},{5,4},{6,7},{7,6},{8,9},{9,8},{10,11... | collective-permute-start | bytes 393224 | tf_op jit(solution)/shard_map/ppermute | solution.py:323
  51.1 5.9 %all-to-all-done.1.sums = f32[8,2,128]{2,1,0:T(2,128)S(1)} async-done(((f32[8,2,128]{2,1,0:T(2,128)}), f32[8,2,128]{2,1,0:T(2,128)S(1)}, u32[]{:S(2)}, u32[]{:S(2)}) %all-to-all-start.1) | async-done | bytes 8224 | tf_op jit(solution)/shard_map/all_to_all | solution.py:322
  57.0 0.3 coef.1.normed
  57.3 0.0 collective-permute-done.refs_0_
  57.3 0.0 collective-permute-done.1.refs_1_
  57.3 1.0 %all-gather.3.cloned.1.call-done = bf16[16,512,128]{2,1,0:T(8,128)(2,1)} async-done(((bf16[2,512,128]{2,1,0:T(8,128)(2,1)}), bf16[16,512,128]{2,1,0:T(8,128)(2,1)}) %all-gather.3.cloned.1.call-update) | async-done | bytes 2097168 | tf_op jit(solution)/shard_map/all_gather | solution.py:309
  58.3 0.0 copy-start
  58.3 1.6 %copy-done = bf16[16,512,128]{2,1,0:T(8,128)(2,1)S(1)} copy-done((bf16[16,512,128]{2,1,0:T(8,128)(2,1)S(1)}, bf16[16,512,128]{2,1,0:T(8,128)(2,1)}, u32[]{:S(2)}) %copy-start) | copy-done | bytes 2097176
  59.9 0.0 copy-start.1
  59.9 1.9 %attend23.1 = (bf16[544,128]{1,0:T(8,128)(2,1)S(1)}, bf16[544,128]{1,0:T(8,128)(2,1)S(1)}, bf16[8,2,256,128]{3,2,1,0:T(8,128)(2,1)S(1)}) custom-call(bf16[8,2,512,128]{3,2,1,0:T(8,128)(2,1)S(1)} %bitcast.11, f32[2,8,2,128,128]{4,3,2,1,0:T(8,128)S(1)} %coef.1.normed, bf16[2,256,128]{2,1,0:T(8,128)(2,1)S(1)} %collective-permute-done.refs_0_, ...), custom_call_target="tpu_custom_call" | custom-call | flops 805306368 | bytes 4000000 | tf_op jit(solution)/shard_map/attend23/pallas_call | solution.py:336
  61.8 4.7 %collective-permute-start.3 = (bf16[544,128]{1,0:T(8,128)(2,1)S(1)}, bf16[544,128]{1,0:T(8,128)(2,1)S(1)}, u32[]{:S(2)}, u32[]{:S(2)}) collective-permute-start(bf16[544,128]{1,0:T(8,128)(2,1)S(1)} %get-tuple-element.29), channel_id=1, source_target_pairs={{0,2},{1,3},{2,0},{3,1},{4,6},{5,7},{6,4},{7,5},{8,10},{9,11},{10,... | collective-permute-start | bytes 417800 | tf_op jit(solution)/shard_map/ppermute | solution.py:323
  66.6 3.1 %collective-permute-start.4 = (bf16[544,128]{1,0:T(8,128)(2,1)S(1)}, bf16[544,128]{1,0:T(8,128)(2,1)S(1)}, u32[]{:S(2)}, u32[]{:S(2)}) collective-permute-start(bf16[544,128]{1,0:T(8,128)(2,1)S(1)} %get-tuple-element.30), channel_id=1, source_target_pairs={{0,3},{1,2},{2,1},{3,0},{4,7},{5,6},{6,5},{7,4},{8,11},{9,10},{10,... | collective-permute-start | bytes 417800 | tf_op jit(solution)/shard_map/ppermute | solution.py:323
  69.7 0.0 collective-permute-done.2.refs_0_
  69.7 0.0 copy-done.1
  69.7 1.4 %attend1.1 = bf16[528,128]{1,0:T(8,128)(2,1)S(1)} custom-call(bf16[8,2,512,128]{3,2,1,0:T(8,128)(2,1)S(1)} %bitcast.12, bf16[8,2,256,128]{3,2,1,0:T(8,128)(2,1)S(1)} %get-tuple-element.27.normed, bf16[2,256,128]{2,1,0:T(8,128)(2,1)S(1)} %collective-permute-done.2.refs_0_), custom_call_target="tpu_custom_call" | custom-call | flops 402653184 | bytes 4000000 | tf_op jit(solution)/shard_map/attend1/pallas_call | solution.py:336
  71.1 2.3 %collective-permute-start.5 = (bf16[528,128]{1,0:T(8,128)(2,1)S(1)}, bf16[528,128]{1,0:T(8,128)(2,1)S(1)}, u32[]{:S(2)}, u32[]{:S(2)}) collective-permute-start(bf16[528,128]{1,0:T(8,128)(2,1)S(1)} %attend1.1), channel_id=1, source_target_pairs={{0,1},{1,0},{2,3},{3,2},{4,5},{5,4},{6,7},{7,6},{8,9},{9,8},{10,11... | collective-permute-start | bytes 405512 | tf_op jit(solution)/shard_map/ppermute | solution.py:323
  73.5 1.4 %attend0.1.p0 = bf16[528,128]{1,0:T(8,128)(2,1)S(1)} custom-call(bf16[8,2,512,128]{3,2,1,0:T(8,128)(2,1)S(1)} %bitcast.13, bf16[8,2,256,128]{3,2,1,0:T(8,128)(2,1)S(1)} %get-tuple-element.27.normed, bf16[2,256,128]{2,1,0:T(8,128)(2,1)S(1)} %get-tuple-element.23.refs_0_), custom_call_target="tpu_custom_call" | custom-call | flops 402653184 | bytes 4000000 | tf_op jit(solution)/shard_map/attend0/pallas_call | solution.py:336
  74.9 0.0 collective-permute-done.3.p2
  74.9 0.7 collective-permute-done.4.p3
  75.6 0.2 three.1
  75.7 2.3 %collective-permute-done.5.last = bf16[528,128]{1,0:T(8,128)(2,1)S(1)} collective-permute-done((bf16[528,128]{1,0:T(8,128)(2,1)S(1)}, bf16[528,128]{1,0:T(8,128)(2,1)S(1)}, u32[]{:S(2)}, u32[]{:S(2)}) %collective-permute-start.5) | collective-permute-done | bytes 135200 | tf_op jit(solution)/shard_map/ppermute | solution.py:323
  78.0 0.8 merge.1
Async XLA Ops:
  7.2 51.1 %all-gather.3.cloned.1.call-start = ((), (), s32[]{:S(2)}) async-start(), calls=%async_computation.2 | async-start | bytes 2359296 | tf_op jit(solution)/shard_map/all_gather | solution.py:309
  32.8 1.0 %copy-start.2 = (f32[2,2,136,128]{3,2,1,0:T(8,128)S(1)}, f32[2,2,136,128]{3,2,1,0:T(8,128)}, u32[]{:S(2)}) copy-start(f32[2,2,136,128]{3,2,1,0:T(8,128)} %get-tuple-element.20.scaled) | copy-start | bytes 835588
  34.4 22.9 %collective-permute-start = (bf16[2,256,128]{2,1,0:T(8,128)(2,1)S(1)}, bf16[2,256,128]{2,1,0:T(8,128)(2,1)S(1)}, u32[]{:S(2)}, u32[]{:S(2)}) collective-permute-start(bf16[2,256,128]{2,1,0:T(8,128)(2,1)S(1)} %get-tuple-element.23.refs_0_), channel_id=1, source_target_pairs={{0,2},{1,3},{2,0},{3,1},{4,6},{5,7},{6,4},{7,5},{8,10},{9,11},{10,... | collective-permute-start | bytes 393224 | tf_op jit(solution)/shard_map/ppermute | solution.py:323
  38.8 18.5 %collective-permute-start.1 = (bf16[2,256,128]{2,1,0:T(8,128)(2,1)S(1)}, bf16[2,256,128]{2,1,0:T(8,128)(2,1)S(1)}, u32[]{:S(2)}, u32[]{:S(2)}) collective-permute-start(bf16[2,256,128]{2,1,0:T(8,128)(2,1)S(1)} %get-tuple-element.23.refs_0_), channel_id=1, source_target_pairs={{0,3},{1,2},{2,1},{3,0},{4,7},{5,6},{6,5},{7,4},{8,11},{9,10},{10,... | collective-permute-start | bytes 393224 | tf_op jit(solution)/shard_map/ppermute | solution.py:323
  42.0 14.9 %all-to-all-start.1 = ((f32[8,2,128]{2,1,0:T(2,128)}), f32[8,2,128]{2,1,0:T(2,128)S(1)}, u32[]{:S(2)}, u32[]{:S(2)}) async-start(f32[8,2,128]{2,1,0:T(2,128)} %get-tuple-element.21), calls=%async_computation.1 | async-start | bytes 16384 | tf_op jit(solution)/shard_map/all_to_all | solution.py:322
  49.2 20.5 %collective-permute-start.2 = (bf16[2,256,128]{2,1,0:T(8,128)(2,1)S(1)}, bf16[2,256,128]{2,1,0:T(8,128)(2,1)S(1)}, u32[]{:S(2)}, u32[]{:S(2)}) collective-permute-start(bf16[2,256,128]{2,1,0:T(8,128)(2,1)S(1)} %get-tuple-element.23.refs_0_), channel_id=1, source_target_pairs={{0,1},{1,0},{2,3},{3,2},{4,5},{5,4},{6,7},{7,6},{8,9},{9,8},{10,11... | collective-permute-start | bytes 393224 | tf_op jit(solution)/shard_map/ppermute | solution.py:323
  58.3 1.6 %copy-start = (bf16[16,512,128]{2,1,0:T(8,128)(2,1)S(1)}, bf16[16,512,128]{2,1,0:T(8,128)(2,1)}, u32[]{:S(2)}) copy-start(bf16[16,512,128]{2,1,0:T(8,128)(2,1)} %all-gather.3.cloned.1.call-done) | copy-start | bytes 6291460
  59.9 9.8 %copy-start.1 = (bf16[16,512,128]{2,1,0:T(8,128)(2,1)S(1)}, bf16[16,512,128]{2,1,0:T(8,128)(2,1)}, u32[]{:S(2)}) copy-start(bf16[16,512,128]{2,1,0:T(8,128)(2,1)} %all-gather.3.cloned.1.call-done) | copy-start | bytes 6291460
  61.8 13.0 %collective-permute-start.3 = (bf16[544,128]{1,0:T(8,128)(2,1)S(1)}, bf16[544,128]{1,0:T(8,128)(2,1)S(1)}, u32[]{:S(2)}, u32[]{:S(2)}) collective-permute-start(bf16[544,128]{1,0:T(8,128)(2,1)S(1)} %get-tuple-element.29), channel_id=1, source_target_pairs={{0,2},{1,3},{2,0},{3,1},{4,6},{5,7},{6,4},{7,5},{8,10},{9,11},{10,... | collective-permute-start | bytes 417800 | tf_op jit(solution)/shard_map/ppermute | solution.py:323
  66.6 9.0 %collective-permute-start.4 = (bf16[544,128]{1,0:T(8,128)(2,1)S(1)}, bf16[544,128]{1,0:T(8,128)(2,1)S(1)}, u32[]{:S(2)}, u32[]{:S(2)}) collective-permute-start(bf16[544,128]{1,0:T(8,128)(2,1)S(1)} %get-tuple-element.30), channel_id=1, source_target_pairs={{0,3},{1,2},{2,1},{3,0},{4,7},{5,6},{6,5},{7,4},{8,11},{9,10},{10,... | collective-permute-start | bytes 417800 | tf_op jit(solution)/shard_map/ppermute | solution.py:323
  71.1 6.9 %collective-permute-start.5 = (bf16[528,128]{1,0:T(8,128)(2,1)S(1)}, bf16[528,128]{1,0:T(8,128)(2,1)S(1)}, u32[]{:S(2)}, u32[]{:S(2)}) collective-permute-start(bf16[528,128]{1,0:T(8,128)(2,1)S(1)} %attend1.1), channel_id=1, source_target_pairs={{0,1},{1,0},{2,3},{3,2},{4,5},{5,4},{6,7},{7,6},{8,9},{9,8},{10,11... | collective-permute-start | bytes 405512 | tf_op jit(solution)/shard_map/ppermute | solution.py:323
Sparse Core Ops, SparseCore 0:
  10.1 48.1 all-gather.2
